TPU v7x, 512 devices: a whole 4x4x16 slice. The times are simulated.
512 devices in a mesh: row: 32 (over z, core), col: 16 (over y, x).
Axes of the slice: x: 4, y: 4, z: 16, core: 2. Of those that a mesh axis runs over, the one named last changes fastest.
Arguments:
- rhs: float32 [32, 1024, 4096], P('row', None, 'col'), may hold values from -6 to 6
- panel: float32 [32, 2, 1024, 1024], P('row', None, 'col'), may hold values from -0.125 to 0.125
- diag_inverse: float32 [2, 1024, 1024], P(None, 'row'), as said below
- flags: int32 [32, 2], P('row'), may hold values 0 or 1
- slot_block: int32 [32], replicated, may hold values from 0 to 31, each once
Outputs:
- result: float32 [32, 1024, 4096], P('row', None, 'col')
Inputs may be any that keep to these rules, and one draw needn't show every extreme that they name: `slot_block`: each block row 0 to 31 is held by exactly one slot. `diag_inverse`: lower triangular with a positive diagonal.
All inputs are finite; a program needn't handle non-finite values. No bound on the sum of `flags` on one device may be relied on, other than what follows from the above.
Results may differ from a plain program's by a relative error of at most 0.000078.
Values sent between devices are 32-bit elements; how exact they have to be, the bound alone decides.
A program may use at most 64 MiB of HBM per device.

v0:
```python
import jax
import jax.numpy as jnp
from jax import lax
from jax.sharding import PartitionSpec as P


def broadcast(shard, axis, root):
    mine = lax.axis_index(axis) == root
    return lax.psum(jnp.where(mine, shard, jnp.zeros_like(shard)), axis)


def shards(rhs, panel, diag_inverse, flags, slot_block):
    highest = lax.Precision.HIGHEST
    rank = lax.axis_index("row")
    held = slot_block[rank]
    owners = (jnp.argmax(slot_block == 0), jnp.argmax(slot_block == 1))
    weights = flags[0].astype(jnp.float32)
    current = rhs[0]
    solved = []
    for step in range(2):
        pivot = broadcast(current, "row", owners[step])
        share = jnp.dot(diag_inverse[step], pivot, precision=highest)
        block_x = lax.all_gather(share, "row", axis=0, tiled=True)
        product = jnp.dot(
            lax.all_gather(panel[0, step], "col", axis=0, tiled=True), block_x, precision=highest
        )
        current = current - weights[step] * product
        solved.append(block_x)
    result = jnp.where(held == 0, solved[0], jnp.where(held == 1, solved[1], current))
    return result[None]


def solution(mesh):
    in_specs = (
        P("row", None, "col"),
        P("row", None, "col", None),
        P(None, "row", None),
        P("row", None),
        P(),
    )
    out_specs = P("row", None, "col")
    return jax.shard_map(shards, mesh=mesh, in_specs=in_specs, out_specs=out_specs, check_vma=False)
```

profile of v0, /device:TPU:1, one launch (start us, length us, event | category | flops | bytes accessed | tf_op | source)
XLA Modules:
  0.0 742.7 jit_solution(17885400860073006473)
XLA Ops:
  6.5 0.0 copy-start.5
  6.5 0.0 copy-start.1
  6.5 0.0 copy-start.2
  6.5 0.0 copy-start.4
  6.5 0.0 all-reduce.3.cloned.1.call-start
  6.6 1.5 compare_reduce_fusion.1
  8.8 2.3 bitcast_select_fusion
  11.1 0.0 all-reduce.3.cloned.1.call-update
  11.1 0.0 all-gather.7.cloned.1.call-start
  11.1 215.9 %all-reduce.3.cloned.1.call-done = f32[1024,256]{1,0:T(8,128)} async-done(((f32[1024,256]{1,0:T(8,128)}), f32[1024,256]{1,0:T(8,128)}) %all-reduce.3.cloned.1.call-update) | async-done | bytes 1048592 | tf_op jit(solution)/shard_map/psum | solution.py:9
  227.0 2.5 convolution_bitcast_fusion.1
  229.5 0.0 all-gather.7.cloned.1.call-update
  229.5 0.0 all-gather.11.cloned.1.call-start
  229.6 0.0 copy-done.2
  229.6 0.8 fusion.35
  230.4 0.0 all-gather.11.cloned.1.call-update
  230.5 0.0 all-reduce.5.cloned.1.call-start
  230.5 0.0 copy-done.5
  230.5 0.7 compare_reduce_fusion
  231.8 0.0 copy-done.4
  231.8 0.6 fusion.36
  232.4 68.0 %all-gather.7.cloned.1.call-done = f32[1024,256]{1,0:T(8,128)} async-done(((f32[32,256]{1,0:T(8,128)}), f32[1024,256]{1,0:T(8,128)}) %all-gather.7.cloned.1.call-update) | async-done | bytes 1048592 | tf_op jit(solution)/shard_map/all_gather | solution.py:23
  300.5 67.1 %all-gather.11.cloned.1.call-done = f32[1,1,1024,1024]{3,2,1,0:T(8,128)} async-done(((f32[1,1,64,1024]{3,2,1,0:T(8,128)}), f32[1,1,1024,1024]{3,2,1,0:T(8,128)}) %all-gather.11.cloned.1.call-update) | async-done | bytes 4194320 | tf_op jit(solution)/shard_map/all_gather | solution.py:25
  367.5 0.0 copy-done.1
  367.6 0.0 copy-start.3
  367.6 0.0 copy-start
  367.6 7.7 %broadcast_select_fusion = (f32[1024,256]{1,0:T(8,128)}, f32[1024,256]{1,0:T(8,128)S(1)}) fusion(pred[]{:T(512)S(6)} %eq.42, f32[1024,256]{1,0:T(8,128)} %all-gather.7.cloned.1.call-done, f32[1,1,1024,1024]{3,2,1,0:T(8,128)} %all-gather.11.cloned.1.call-done, f32[]{:T(128)} %bitcast.5, f32[1,1024,256]{2,1,0:T(8,128)S(1)} %copy-done.1), kind=kOutput, calls=%fused_computation.16 | convolution fusion | flops 3222011904 | bytes 8388613 | tf_op jit(solution)/shard_map/dot_general | solution.py:24
  375.3 0.0 all-reduce.5.cloned.1.call-update
  375.3 0.0 all-gather.13.cloned.1.call-start
  375.3 0.5 all-gather.13.cloned.1.call-update
  375.9 0.0 all-gather.9.cloned.1.call-start
  375.9 209.8 %all-reduce.5.cloned.1.call-done = f32[1024,256]{1,0:T(8,128)} async-done(((f32[1024,256]{1,0:T(8,128)}), f32[1024,256]{1,0:T(8,128)}) %all-reduce.5.cloned.1.call-update) | async-done | bytes 1048592 | tf_op jit(solution)/shard_map/psum | solution.py:9
  585.7 0.0 copy-done.3
  585.7 2.5 convolution_bitcast_fusion
  588.2 0.0 all-gather.9.cloned.1.call-update
  588.2 0.6 dynamic_slice.3
  590.1 65.0 %all-gather.13.cloned.1.call-done = f32[1,1,1024,1024]{3,2,1,0:T(8,128)} async-done(((f32[1,1,64,1024]{3,2,1,0:T(8,128)}), f32[1,1,1024,1024]{3,2,1,0:T(8,128)}) %all-gather.13.cloned.1.call-update) | async-done | bytes 4194320 | tf_op jit(solution)/shard_map/all_gather | solution.py:25
  655.2 72.9 %all-gather.9.cloned.1.call-done = f32[1024,256]{1,0:T(8,128)} async-done(((f32[32,256]{1,0:T(8,128)}), f32[1024,256]{1,0:T(8,128)}) %all-gather.9.cloned.1.call-update) | async-done | bytes 1048592 | tf_op jit(solution)/shard_map/all_gather | solution.py:23
  728.0 0.0 copy-done
  728.0 7.9 %fusion.28 = f32[1,1024,256]{2,1,0:T(8,128)} fusion(f32[1024,256]{1,0:T(8,128)S(1)} %copy-done, f32[1024,256]{1,0:T(8,128)} %all-gather.9.cloned.1.call-done, f32[1024,256]{1,0:T(8,128)S(1)} %get-tuple-element.14, f32[1,1,1024,1024]{3,2,1,0:T(8,128)} %all-gather.13.cloned.1.call-done, f32[]{:T(128)} %bitcast.10, pred[]{:T(512)} %bitcast.4, pred[]{:T(512)} %bitcast), kind=kOutput, calls=%fused_computation.12 | convolution fusion | flops 3222274048 | bytes 8388614 | tf_op jit(solution)/shard_map/dot_general | solution.py:24
  (1 shorter events, 0.0 us)
Async XLA Ops:
  6.5 224.0 %copy-start.5 = (s32[32]{0:T(128)S(1)}, s32[32]{0:T(128)}, u32[]{:S(2)}) copy-start(s32[32]{0:T(128)} %param.9) | copy-start | bytes 388
  6.5 361.0 %copy-start.1 = (f32[1,1024,256]{2,1,0:T(8,128)S(1)}, f32[1,1024,256]{2,1,0:T(8,128)}, u32[]{:S(2)}) copy-start(f32[1,1024,256]{2,1,0:T(8,128)} %param.5) | copy-start | bytes 3145732
  6.5 223.1 %copy-start.2 = (f32[1,2,64,1024]{3,2,1,0:T(8,128)S(1)}, f32[1,2,64,1024]{3,2,1,0:T(8,128)}, u32[]{:S(2)}) copy-start(f32[1,2,64,1024]{3,2,1,0:T(8,128)} %param.6) | copy-start | bytes 1572868
  6.5 225.3 %copy-start.4 = (s32[1,2]{1,0:T(1,128)S(1)}, s32[1,2]{1,0:T(1,128)}, u32[]{:S(2)}) copy-start(s32[1,2]{1,0:T(1,128)} %param.8) | copy-start | bytes 28
  6.5 220.5 %all-reduce.3.cloned.1.call-start = ((), (), s32[]{:S(2)}) async-start(), calls=%async_computation | async-start | bytes 2097152 | tf_op jit(solution)/shard_map/psum | solution.py:9
  11.1 289.4 %all-gather.7.cloned.1.call-start = ((), (), s32[]{:S(2)}) async-start(), calls=%async_computation.1 | async-start | bytes 1081344 | tf_op jit(solution)/shard_map/all_gather | solution.py:23
  229.5 138.0 %all-gather.11.cloned.1.call-start = ((), (), s32[]{:S(2)}) async-start(), calls=%async_computation.4 | async-start | bytes 4456448 | tf_op jit(solution)/shard_map/all_gather | solution.py:25
  230.5 355.3 %all-reduce.5.cloned.1.call-start = ((), (), s32[]{:S(2)}) async-start(), calls=%async_computation.2 | async-start | bytes 2097152 | tf_op jit(solution)/shard_map/psum | solution.py:9
  367.6 218.2 %copy-start.3 = (f32[2,32,1024]{2,1,0:T(8,128)S(1)}, f32[2,32,1024]{2,1,0:T(8,128)}, u32[]{:S(2)}) copy-start(f32[2,32,1024]{2,1,0:T(8,128)} %param.7) | copy-start | bytes 786436
  367.6 360.5 %copy-start = (f32[1024,256]{1,0:T(8,128)S(1)}, f32[1024,256]{1,0:T(8,128)}, u32[]{:S(2)}) copy-start(f32[1024,256]{1,0:T(8,128)} %all-gather.7.cloned.1.call-done) | copy-start | bytes 3145732
  375.3 279.9 %all-gather.13.cloned.1.call-start = ((), (), s32[]{:S(2)}) async-start(), calls=%async_computation.5 | async-start | bytes 4456448 | tf_op jit(solution)/shard_map/all_gather | solution.py:25
  375.9 352.1 %all-gather.9.cloned.1.call-start = ((), (), s32[]{:S(2)}) async-start(), calls=%async_computation.3 | async-start | bytes 1081344 | tf_op jit(solution)/shard_map/all_gather | solution.py:23
Sparse Core Ops, SparseCore 0:
  11.2 215.8 all-reduce.2
  229.7 70.7 all-gather.6
  303.9 63.5 all-gather.10
  375.4 210.2 all-reduce.4
  588.6 66.5 all-gather.12
  657.1 70.8 all-gather.8
where the time goes:
time: 743 us
  waiting for transfers between devices  699 us (94%)
  matrix products  20.5 us (3%)
  between operations  16.1 us (2%)
    psum x2, waiting for transfers between devices, broadcast(): return lax.psum(jnp.where(mine, shard, jnp.zeros_like(shard)), axis)  426 us
    all_gather x2, waiting for transfers between devices, shards(): block_x = lax.all_gather(share, 'row', axis=0, tiled=True)  141 us
    all_gather x2, waiting for transfers between devices, shards(): lax.all_gather(panel[0, step], 'col', axis=0, tiled=True)  132 us
    dot_general x2, matrix products, shards(): jnp.dot(lax.all_gather(panel[0, step], 'col', axis=0, tiled=True), block_...  15.6 us
  transfers between devices with their start and end apart: 6, of which 6 were waited for; matrix products, arithmetic and copies ran while one was open for 1% of the time, Pallas kernels for 0%

commit v1 on v0

v1 whole, which is shorter than its diff:
```python
import jax
import jax.numpy as jnp
from jax import lax
from jax.experimental import pallas as pl
from jax.experimental.pallas import tpu as pltpu
from jax.sharding import PartitionSpec as P

MESH = pl.DeviceIdType.MESH
F32 = jnp.float32
BF16 = jnp.bfloat16
Z = 16
S = 4


def split(a):
    high = a.astype(BF16)
    return high, (a - high.astype(F32)).astype(BF16)


def dot(a, b):
    return jnp.dot(a, b, preferred_element_type=F32)


def dot3(a, b_high, b_low):
    a_high, a_low = split(a)
    return dot(a_high, b_high) + (dot(a_high, b_low) + dot(a_low, b_high))


class Copy:
    def __init__(self, make):
        self.make = make

    def op(self):
        src, dst, send, recv, device = self.make()
        return pltpu.make_async_remote_copy(
            src_ref=src, dst_ref=dst, send_sem=send, recv_sem=recv, device_id=device, device_id_type=MESH
        )

    def start(self):
        self.op().start()

    def sent(self):
        self.op().wait_send()

    def came(self):
        self.op().wait_recv()


class Plane:
    def __init__(self, place, a, b, send, recv, base=0):
        self.r, self.y, self.x = place
        self.a, self.b, self.send, self.recv, self.base = a, b, send, recv, base
        self.sends = []

    def copy(self, n, piece, place, dx, dy):
        def make():
            y, x = lax.rem(self.y + dy + S, S), lax.rem(self.x + dx + S, S)
            view = piece(*self.at(*place))
            return view, view, self.send.at[self.base + n], self.recv.at[self.base + n], (self.r, y * S + x)
        return Copy(make)

    def at(self, dy, dx, part):
        y = None if dy is None else lax.rem(self.y + dy, S)
        x = None if dx is None else lax.rem(self.x + dx, S)
        return y, x, part

    def put(self, n, piece, place, dx, dy):
        copy = self.copy(n, piece, place, dx, dy)
        copy.start()
        self.sends.append(copy)

    def got(self, n, piece, place):
        self.copy(n, piece, place, 0, 0).came()

    def a0(self):
        self.put(0, self.a, (0, 0, 0), 1, 0)
        self.put(1, self.a, (0, 0, 0), -1, 0)
        self.put(2, self.b, (0, 0, 0), 0, 1)
        self.put(3, self.b, (0, 0, 0), 0, -1)

    def a1(self):
        self.got(0, self.a, (0, 3, 0))
        self.put(4, self.a, (0, 3, 1), 1, 0)
        self.got(2, self.b, (3, 0, 0))
        self.put(6, self.b, (3, 0, 1), 0, 1)
        self.got(1, self.a, (0, 1, 0))
        self.put(5, self.a, (0, 1, 2), -1, 0)
        self.got(3, self.b, (1, 0, 0))
        self.put(7, self.b, (1, 0, 2), 0, -1)

    def b0(self):
        self.got(4, self.a, (0, 2, 1))
        self.got(5, self.a, (0, 2, 2))
        self.put(8, self.a, (0, None, 0), 0, 1)
        self.put(9, self.a, (0, None, 0), 0, -1)
        self.got(6, self.b, (2, 0, 1))
        self.got(7, self.b, (2, 0, 2))
        self.put(10, self.b, (None, 0, 0), 1, 0)
        self.put(11, self.b, (None, 0, 0), -1, 0)

    def b1(self):
        self.got(8, self.a, (3, None, 0))
        self.put(12, self.a, (3, None, 1), 0, 1)
        self.got(10, self.b, (None, 3, 0))
        self.put(14, self.b, (None, 3, 1), 1, 0)
        self.got(9, self.a, (1, None, 0))
        self.put(13, self.a, (1, None, 2), 0, -1)
        self.got(11, self.b, (None, 1, 0))
        self.put(15, self.b, (None, 1, 2), -1, 0)

    def end(self):
        self.got(12, self.a, (2, None, 1))
        self.got(13, self.a, (2, None, 2))
        self.got(14, self.b, (None, 2, 1))
        self.got(15, self.b, (None, 2, 2))

    def sent(self):
        for copy in self.sends:
            copy.sent()


class Gather:
    def __init__(self, z, q, c, buf, send, recv):
        self.z, self.q, self.c, self.buf, self.send, self.recv = z, q, c, buf, send, recv
        self.sends = []

    def copy(self, n, chunk, dz):
        def make():
            to = lax.rem(self.z + dz + Z, Z)
            view = self.buf.at[lax.rem(self.z + chunk + Z, Z)]
            return view, view, self.send.at[n], self.recv.at[n], (to * 2 + self.q, self.c)
        return Copy(make)

    def put(self, n, chunk, dz):
        copy = self.copy(n, chunk, dz)
        copy.start()
        self.sends.append(copy)

    def got(self, n, chunk):
        self.copy(n, chunk, 0).came()

    def first(self):
        self.put(0, 0, 2)
        self.put(8, 0, -2)
        self.put(4, 0, 1)
        self.put(11, 0, -1)

    def step(self, k):
        self.got(k - 1, -2 * k)
        self.put(k, -2 * k, 2)
        self.put(4 + k, -2 * k, 1)
        self.got(8 + k - 1, 2 * k)
        if k < 3:
            self.put(8 + k, 2 * k, -2)
        self.put(11 + k, 2 * k, -1)

    def end(self):
        self.got(3, -8)
        for k in range(4):
            self.got(4 + k, -2 * k - 1)
            self.got(11 + k, 2 * k + 1)

    def sent(self):
        for copy in self.sends:
            copy.sent()


def kernel(
    slot_ref, flag_ref, rhs_ref, panel_ref, diag_ref, out_ref,
    full, low, mine0, other0, mine1, other1, even_r, odd_r, even_l, odd_l, hop_r, hop_l,
    ez, ea, eb, ea0, eb0, p10, b0, b1c, b1, x0, x1, xh, xl, wh, wl,
    p_send, p_recv, e_send, e_recv, t_send, t_recv, r0_send, r0_recv, g0_send, g0_recv,
    r1_send, r1_recv, g1_send, g1_recv, m_send, m_recv, z_send, z_recv, z_self, f_send, f_recv,
):
    r, c = lax.axis_index("row"), lax.axis_index("col")
    z, q = r // 2, lax.rem(r, 2)
    y, x = c // S, lax.rem(c, S)
    pair = (z * 2 + 1 - q, c)

    def turn(a, n):
        return lax.rem(a + 2 * n, n)

    barrier = pltpu.get_barrier_semaphore()

    def hello(device):
        pl.semaphore_signal(barrier, inc=1, device_id=device, device_id_type=MESH)

    for dy, dx in ((0, 1), (0, -1), (1, 0), (-1, 0)):
        hello((r, turn(y + dy, S) * S + turn(x + dx, S)))
    hello(pair)
    for d in (1, 2, 3, 4):
        for dz in (d, -d):
            for core in range(2):
                hello((turn(z + dz, Z) * 2 + core, c))

    held = slot_ref[r]
    is0 = jnp.where(held == 0, 1.0, 0.0).astype(F32)
    is1 = jnp.where(held == 1, 1.0, 0.0).astype(F32)
    f0 = flag_ref[0, 0].astype(F32)
    f1 = flag_ref[0, 1].astype(F32)

    def keep(mark, a, b):
        return jnp.where(jnp.full(a.shape, mark, F32) > 0.5, a, b)

    def mask0(d, _):
        j = lax.rem(z + d, Z)
        rows = rhs_ref[pl.ds(pl.multiple_of(j * 64, 64), 64), :]
        mine0[d, 0:64, :] = keep(is0, rows, jnp.zeros_like(rows))
        t = j // 2
        block = panel_ref[0, pl.ds(pl.multiple_of(t * 8, 8), 8), :] * f0
        block = keep(is1, block, jnp.zeros_like(block))
        for a in range(4):
            mine0[d, 64 + 8 * a : 72 + 8 * a, :] = block[:, 256 * a : 256 * a + 256]
        return 0

    def mask1(d, _):
        j = lax.rem(z + d, Z)
        t, h = j // 2, lax.rem(j, 2)
        for k in range(16):
            rows = rhs_ref[pl.ds(pl.multiple_of(64 * k + t * 8, 8), 8), pl.ds(pl.multiple_of(h * 128, 128), 128)]
            mine1[d, 8 * k : 8 * k + 8, :] = keep(is1, rows, jnp.zeros_like(rows))
        return 0

    lax.fori_loop(0, Z, mask0, 0)
    for k in range(2):
        full[k, y, x] = panel_ref[k]

    pl.semaphore_wait(barrier, 21)

    place = (r, y, x)

    def half(lo, hi):
        def view(k):
            def piece(yy, xx, part):
                mid = (lo + hi) // 2
                rows = pl.ds(*((lo, hi - lo), (lo, mid - lo), (mid, hi - mid))[part])
                yy = slice(None) if yy is None else yy
                xx = slice(None) if xx is None else xx
                return full.at[k, yy, xx, rows, :]
            return piece
        return view

    top, bottom = half(0, 32), half(32, 64)
    panels = [Plane(place, top(k), bottom(k), p_send, p_recv, 16 * k) for k in range(2)]

    def columns(buf, lo, hi):
        def piece(yy, xx, part):
            mid = (lo + hi) // 2
            cols = pl.ds(*((lo, hi - lo), (lo, mid - lo), (mid, hi - mid))[part])
            yy = slice(None) if yy is None else yy
            xx = slice(None) if xx is None else xx
            return buf.at[yy, xx, :, cols]
        return piece

    diag = Plane(place, columns(ea, 0, 2560), columns(eb, 0, 2560), e_send, e_recv)
    tenth = Plane(place, columns(p10, 0, 512), columns(p10, 512, 1024), t_send, t_recv)
    gather0 = Gather(z, q, c, b0, g0_send, g0_recv)
    gather1 = Gather(z, q, c, b1c, g1_send, g1_recv)

    panels[0].a0()

    groups = ((6, 5), (11, 5), (0, 6))
    merges = [
        Copy(lambda i=i, g=g: (mine0.at[pl.ds(*g)], other0.at[pl.ds(*g)], m_send.at[i], m_recv.at[i], pair))
        for i, g in enumerate(groups)
    ]
    merges.append(Copy(lambda: (mine1, other1, m_send.at[3], m_recv.at[3], pair)))

    @pl.when(q == 0)
    def _():
        for copy in merges[:3]:
            copy.start()

    lax.fori_loop(0, Z, mask1, 0)

    @pl.when(q == 0)
    def _():
        merges[3].start()

    reduce0 = []
    reduce1 = []

    def send0(n, d, to, buf, i):
        copy = Copy(lambda: (mine0.at[d % Z], buf.at[i], r0_send.at[n], r0_recv.at[n], (turn(z + to, Z) * 2 + q, c)))
        copy.start()
        reduce0.append(copy)

    def recv0(n, buf, i):
        Copy(lambda: (buf.at[i], buf.at[i], r0_send.at[n], r0_recv.at[n], (r, c))).came()

    def merge0(i):
        merges[i].came()
        lo, n = groups[i]
        for d in range(lo, lo + n):
            mine0[d] += other0[d]

    def send1(n, d, to, buf, i):
        copy = Copy(lambda: (mine1.at[d % Z], buf.at[i], r1_send.at[n], r1_recv.at[n], (turn(z + to, Z) * 2 + q, c)))
        copy.start()
        reduce1.append(copy)

    def recv1(n, buf, i):
        Copy(lambda: (buf.at[i], buf.at[i], r1_send.at[n], r1_recv.at[n], (r, c))).came()

    def hop(t):
        if t:
            recv1(t - 1, hop_r, t - 1)
            mine1[8 - t] += hop_r[t - 1]
        if t < 8:
            send1(t, 8 - t, 1, hop_r, t)
        if 0 < t < 8:
            recv1(8 + t - 1, hop_l, t - 1)
            mine1[(t - 7) % Z] += hop_l[t - 1]
        if t < 7:
            send1(8 + t, t - 7, -1, hop_l, t)

    @pl.when(q == 1)
    def _():
        merge0(0)
        send0(0, 8, 2, even_r, 0)
        send0(4, 7, 1, odd_r, 0)
        send0(11, -7, -1, odd_l, 0)
        merge0(1)
        merge0(2)
        for i, d in ((1, 5), (2, 3), (3, 1)):
            send0(4 + i, d, 1, odd_r, i)
            send0(11 + i, -d, -1, odd_l, i)
        recv0(11, odd_l, 0)
        mine0[10] += odd_l[0]
        send0(8, -6, -2, even_l, 0)

    fold = (z // 2 + 1) // 2
    target = lax.rem(fold, 2)
    slot = z // 4
    holds = jnp.logical_and(lax.rem(z, 2) == c // 8, q == lax.rem(c // 4, 2))
    def rows():
        return diag_ref.at[:, pl.ds(pl.multiple_of(lax.rem(c, 4) * 8, 8), 8), :]

    spread = []
    for n, dz in enumerate((4, -4, 3, -3, 2, -2, 1, -1)):
        spread.append(Copy(lambda n=n, dz=dz: (rows(), ez.at[slot], z_send.at[n], z_recv.at[slot], (turn(z + dz, Z) * 2 + target, c))))
    across = Copy(lambda: (rows(), ez.at[slot], z_send.at[8], z_recv.at[slot], pair))

    @pl.when(holds)
    def _():
        for copy in spread:
            copy.start()

        @pl.when(target == q)
        def _():
            pltpu.make_async_copy(rows(), ez.at[slot], z_recv.at[slot]).start()

        @pl.when(target != q)
        def _():
            across.start()

    panels[1].a0()

    @pl.when(q == 1)
    def _():
        recv0(0, even_r, 0)
        recv0(4, odd_r, 0)
        mine0[6] += even_r[0] + odd_r[0]
        send0(1, 6, 2, even_r, 1)
        recv0(8, even_l, 0)
        recv0(12, odd_l, 1)
        mine0[12] += even_l[0] + odd_l[1]
        send0(9, -4, -2, even_l, 1)
        merges[3].came()
        mine1[...] += other1[...]
        hop(0)

    panels[0].a1()

    def wait_slot(m):
        Copy(lambda: (ez.at[m], ez.at[m], z_send.at[0], z_recv.at[m], (r, c))).came()

    relays = []
    for base, step, reach in ((9, 1, (4, 3, 2, 1)), (13, -1, (3, 2, 1))):
        origin = turn(z - 4 * step, Z)
        serves = jnp.logical_and(lax.rem(origin, 2) == c // 8, lax.rem((origin // 2 + 1) // 2, 2) == q)
        m = origin // 4
        copies = [
            Copy(lambda n=base + i, m=m, dz=step * d: (ez.at[m], ez.at[m], z_send.at[n], z_recv.at[m], (turn(z + dz, Z) * 2 + q, c)))
            for i, d in enumerate(reach)
        ]
        relays.append((serves, copies))

        @pl.when(serves)
        def _(m=m, copies=copies):
            wait_slot(m)
            for copy in copies:
                copy.start()

    @pl.when(q == 1)
    def _():
        recv0(1, even_r, 1)
        recv0(5, odd_r, 1)
        mine0[4] += even_r[1] + odd_r[1]
        send0(2, 4, 2, even_r, 2)
        recv0(9, even_l, 1)
        recv0(13, odd_l, 2)
        mine0[14] += even_l[1] + odd_l[2]
        send0(10, -2, -2, even_l, 2)
        hop(1)

    panels[0].b0()

    for m in range(4):
        origin = 2 * (2 * m + lax.rem(q + m, 2)) + c // 8
        away = turn(origin - z, Z)
        waited = jnp.logical_or(away == 4, away == 12)

        @pl.when(jnp.logical_not(waited))
        def _(m=m):
            wait_slot(m)

    for k in range(2):
        o = 1280 * k
        ea[y, x, :, o : o + 256] = ez[0, k, :, 0:256]
        ea[y, x, :, o + 256 : o + 1280] = ez[3, k, :, :]
        eb[y, x, :, o : o + 512] = ez[1, k, :, 0:512]
        eb[y, x, :, o + 512 : o + 1280] = ez[2, k, :, 0:768]
    diag.a0()

    @pl.when(q == 1)
    def _():
        recv0(2, even_r, 2)
        recv0(6, odd_r, 2)
        mine0[2] += even_r[2] + odd_r[2]
        send0(3, 2, 2, even_r, 3)
        hop(2)

    panels[1].a1()

    @pl.when(q == 1)
    def _():
        recv0(3, even_r, 3)
        recv0(7, odd_r, 3)
        recv0(10, even_l, 2)
        recv0(14, odd_l, 3)
        total = mine0[0] + ((even_r[3] + odd_r[3]) + (even_l[2] + odd_l[3]))
        b0[z] = total[0:64]
        gather0.first()
        for a in range(4):
            p10[y, x, :, 256 * a : 256 * a + 256] = total[64 + 8 * a : 72 + 8 * a]
        tenth.a0()
        hop(3)

    diag.a1()

    @pl.when(q == 1)
    def _():
        gather0.step(1)
        tenth.a1()
        hop(4)

    diag.b0()
    panels[0].b1()

    @pl.when(q == 1)
    def _():
        gather0.step(2)
        tenth.b0()
        hop(5)

    diag.b1()

    @pl.when(q == 1)
    def _():
        gather0.step(3)
        tenth.b1()
        hop(6)

    panels[1].b0()
    panels[0].end()
    diag.end()

    def put_pair(n, src, dst):
        return Copy(lambda: (src, dst, f_send.at[n], f_recv.at[n], pair))

    gifts = [put_pair(0, ea, ea0), put_pair(1, eb, eb0)]

    @pl.when(q == 0)
    def _():
        for copy in gifts:
            copy.start()

    first = [put_pair(2, x0, x0)]
    second = [put_pair(3 + i, x1.at[pl.ds(256 * i, 256)], x1.at[pl.ds(256 * i, 256)]) for i in range(4)]

    def solve(step, source, target_ref, after):
        for b in range(8):
            m, core = b // 2, (b // 2 + b) % 2
            buf, base = (((ea0, ea), 0), ((eb0, eb), 0), ((eb0, eb), 512), ((ea0, ea), 256))[m]
            base += 1280 * step
            width = 128 * (b + 1)
            part = buf[core][:, :, :, base : base + width].reshape(128, width)
            target_ref[128 * b : 128 * b + 128, :] = dot3(part, xh[0:width, :], xl[0:width, :])
            after(b)

    def take(ref):
        for i in range(4):
            high, low_part = split(ref[256 * i : 256 * i + 256, :])
            xh[256 * i : 256 * i + 256, :] = high
            xl[256 * i : 256 * i + 256, :] = low_part

    @pl.when(q == 1)
    def _():
        gather0.end()
        for i in range(16):
            high, low_part = split(b0[i])
            xh[64 * i : 64 * i + 64, :] = high
            xl[64 * i : 64 * i + 64, :] = low_part
        for copy in gifts:
            copy.came()
        solve(0, b0, x0, lambda b: None)
        first[0].start()
        take(x0)
        tenth.end()
        hop(7)
        hop(8)
        h = pl.multiple_of(lax.rem(z, 2) * 128, 128)
        rows1 = mine1[0]
        product = dot3(p10[...].reshape(128, 1024), xh[:, pl.ds(h, 128)], xl[:, pl.ds(h, 128)])
        b1c[z] = rows1 - product
        gather1.first()

    @pl.when(q == 0)
    def _():
        first[0].came()
        take(x0)

    def piece0(i):
        rows_ = slice(256 * i, 256 * i + 256)
        product = dot3(full[0, i].reshape(256, 1024), xh[...], xl[...])
        out_ref[rows_, :] = rhs_ref[rows_, :] - f0 * product

    piece0(0)

    @pl.when(q == 1)
    def _():
        gather1.step(1)

    panels[1].b1()
    piece0(1)

    @pl.when(q == 1)
    def _():
        gather1.step(2)

    piece0(2)

    @pl.when(q == 1)
    def _():
        gather1.step(3)

    piece0(3)
    panels[1].end()

    def split_panel(i):
        high, low_part = split(full[1, i].reshape(256, 1024))
        wh[256 * i : 256 * i + 256, :] = high
        wl[256 * i : 256 * i + 256, :] = low_part

    for i in range(4):
        split_panel(i)

    @pl.when(q == 1)
    def _():
        gather1.end()
        for t in range(8):
            for h in range(2):
                for k in range(16):
                    b1[64 * k + 8 * t : 64 * k + 8 * t + 8, 128 * h : 128 * h + 128] = b1c[2 * t + h, 8 * k : 8 * k + 8, :]
        take(b1)

        def after(b):
            if b % 2:
                second[b // 2].start()

        solve(1, b1, x1, after)

    @pl.when(q == 0)
    def _():
        for copy in second:
            copy.came()

    take(x1)
    for i in range(4):
        rows_ = slice(256 * i, 256 * i + 256)
        product = dot(wh[rows_, :], xh[...]) + (dot(wh[rows_, :], xl[...]) + dot(wl[rows_, :], xh[...]))
        value = out_ref[rows_, :] - f1 * product
        out_ref[rows_, :] = keep(is0, x0[rows_, :], keep(is1, x1[rows_, :], value))

    for gather in panels + [diag]:
        gather.sent()

    @pl.when(q == 0)
    def _():
        for copy in merges + gifts:
            copy.sent()

    @pl.when(q == 1)
    def _():
        tenth.sent()
        for copy in reduce0 + reduce1 + first + second:
            copy.sent()
        gather0.sent()
        gather1.sent()

    @pl.when(holds)
    def _():
        for copy in spread:
            copy.sent()

        @pl.when(target != q)
        def _():
            across.sent()

    for serves, copies in relays:

        @pl.when(serves)
        def _(copies=copies):
            for copy in copies:
                copy.sent()


def shards(rhs, panel, diag_inverse, flags, slot_block):
    vmem = lambda *shape, dtype=F32: pltpu.VMEM(shape, dtype)
    dma = lambda *shape: pltpu.SemaphoreType.DMA(shape)
    scratch = [
        vmem(2, 4, 4, 64, 1024),
        vmem(8, 128),
        vmem(16, 96, 256),
        vmem(16, 96, 256),
        vmem(16, 128, 128),
        vmem(16, 128, 128),
        vmem(4, 96, 256),
        vmem(4, 96, 256),
        vmem(3, 96, 256),
        vmem(4, 96, 256),
        vmem(8, 128, 128),
        vmem(7, 128, 128),
        vmem(4, 2, 8, 1024),
        vmem(4, 4, 8, 2560),
        vmem(4, 4, 8, 2560),
        vmem(4, 4, 8, 2560),
        vmem(4, 4, 8, 2560),
        vmem(4, 4, 8, 1024),
        vmem(16, 64, 256),
        vmem(16, 128, 128),
        vmem(1024, 256),
        vmem(1024, 256),
        vmem(1024, 256),
        vmem(1024, 256, dtype=BF16),
        vmem(1024, 256, dtype=BF16),
        vmem(1024, 1024, dtype=BF16),
        vmem(1024, 1024, dtype=BF16),
        dma(32), dma(32), dma(16), dma(16), dma(16), dma(16),
        dma(15), dma(15), dma(15), dma(15),
        dma(15), dma(15), dma(15), dma(15),
        dma(4), dma(4), dma(16), dma(4), dma(1), dma(7), dma(7),
    ]
    whole = pl.BlockSpec(memory_space=pltpu.VMEM)
    scalar = pl.BlockSpec(memory_space=pltpu.SMEM)
    result = pl.pallas_call(
        kernel,
        out_shape=jax.ShapeDtypeStruct((1024, 256), F32),
        in_specs=[scalar, scalar, whole, whole, whole],
        out_specs=whole,
        scratch_shapes=scratch,
        name="substitution",
        compiler_params=pltpu.CompilerParams(collective_id=0, has_side_effects=True, vmem_limit_bytes=56 << 20),
    )(slot_block, flags, rhs[0], panel[0], diag_inverse)
    return result[None]


def solution(mesh):
    in_specs = (
        P("row", None, "col"),
        P("row", None, "col", None),
        P(None, "row", None),
        P("row", None),
        P(),
    )
    out_specs = P("row", None, "col")
    return jax.shard_map(shards, mesh=mesh, in_specs=in_specs, out_specs=out_specs, check_vma=False)
```

time: 743 us -> 100 us (0.13)
  waiting for transfers between devices: 699 us -> 0 us
  Pallas kernels: 0 us -> 97.9 us
  matrix products: 20.5 us -> 0 us
  between operations: 16.1 us -> 0.01 us
    psum x2 -> x0, waiting for transfers between devices: 426 us -> none  [broadcast(): return lax.psum(jnp.where(mine, shard, jnp.zeros_like(shard)), axis)]
    all_gather x4 -> x0, waiting for transfers between devices: 273 us -> none  [the longest x2 141 us: shards(): block_x = lax.all_gather(share, 'row', axis=0, tiled=True)]
    pallas_call x0 -> x1, Pallas kernels: none -> 97.9 us  [shards(): pl.pallas_call(kernel, out_shape=jax.ShapeDtypeStruct((1024, 256), F32),...]
    dot_general x4 -> x0, matrix products: 20.5 us -> none  [the longest x2 15.6 us: shards(): jnp.dot(lax.all_gather(panel[0, step], 'col', axis=0, tiled=True), block_...]
  transfers between devices with their start and end apart: 6 -> 0, of which waited for: 6 -> 0; matrix products, arithmetic and copies ran while one was open for 1% -> 0% of each run, Pallas kernels for 0% -> 0%
where the time goes in v1:
time: 100 us
  Pallas kernels  97.9 us (98%)
  local copies, waits for them, and re-layouts  2.26 us (2%)
    pallas_call x1, Pallas kernels, shards(): pl.pallas_call(kernel, out_shape=jax.ShapeDtypeStruct((1024, 256), F32),...  97.9 us
    unnamed x1, local copies, waits for them, and re-layouts  2.26 us

profile of v1, /device:TPU:1, one launch (start us, length us, event | category | flops | bytes accessed | tf_op | source)
XLA Modules:
  0.0 100.1 jit_solution(16827796547453816518)
XLA Ops:
  0.0 97.9 %substitution.1 = f32[1024,256]{1,0:T(8,128)} custom-call(s32[32]{0:T(128)} %slot_ref.1, s32[1,2]{1,0:T(1,128)} %flag_ref.1, f32[1024,256]{1,0:T(8,128)} %bitcast.4, f32[2,64,1024]{2,1,0:T(8,128)} %bitcast.5, f32[2,32,1024]{2,1,0:T(8,128)} %diag_ref.1), custom_call_target="tpu_custom_call" | custom-call | tf_op jit(solution)/shard_map/substitution/pallas_call | solution.py:667
  97.9 2.3 %copy.7 = f32[1,1024,256]{2,1,0:T(8,128)} copy(f32[1,1024,256]{2,1,0:T(8,128)} %bitcast.3) | data formatting | bytes 2097152

commit v2 on v0

v2 whole, which is shorter than its diff:
```python
import jax
import jax.numpy as jnp
from jax import lax
from jax.experimental import pallas as pl
from jax.experimental.pallas import tpu as pltpu
from jax.sharding import PartitionSpec as P

MESH = pl.DeviceIdType.MESH
F32 = jnp.float32
BF16 = jnp.bfloat16
Z = 16
S = 4


def split(a):
    high = a.astype(BF16)
    return high, (a - high.astype(F32)).astype(BF16)


def dot(a, b):
    return jnp.dot(a, b, preferred_element_type=F32)


def dot3(a, b_high, b_low):
    a_high, a_low = split(a)
    return dot(a_high, b_high) + (dot(a_high, b_low) + dot(a_low, b_high))


class Copy:
    def __init__(self, make):
        self.make = make

    def op(self):
        src, dst, send, recv, device = self.make()
        return pltpu.make_async_remote_copy(
            src_ref=src, dst_ref=dst, send_sem=send, recv_sem=recv, device_id=device, device_id_type=MESH
        )

    def start(self):
        self.op().start()

    def sent(self):
        self.op().wait_send()

    def came(self):
        self.op().wait_recv()


class Plane:
    def __init__(self, place, a, b, send, recv, base=0):
        self.r, self.y, self.x = place
        self.a, self.b, self.send, self.recv, self.base = a, b, send, recv, base
        self.sends = []

    def copy(self, n, piece, place, dx, dy):
        def make():
            y, x = lax.rem(self.y + dy + S, S), lax.rem(self.x + dx + S, S)
            view = piece(*self.at(*place))
            return view, view, self.send.at[self.base + n], self.recv.at[self.base + n], (self.r, y * S + x)
        return Copy(make)

    def at(self, dy, dx, part):
        y = None if dy is None else lax.rem(self.y + dy, S)
        x = None if dx is None else lax.rem(self.x + dx, S)
        return y, x, part

    def put(self, n, piece, place, dx, dy):
        copy = self.copy(n, piece, place, dx, dy)
        copy.start()
        self.sends.append(copy)

    def got(self, n, piece, place):
        self.copy(n, piece, place, 0, 0).came()

    def a0(self):
        self.put(0, self.a, (0, 0, 0), 1, 0)
        self.put(1, self.a, (0, 0, 0), -1, 0)
        self.put(2, self.b, (0, 0, 0), 0, 1)
        self.put(3, self.b, (0, 0, 0), 0, -1)

    def a1(self):
        self.got(0, self.a, (0, 3, 0))
        self.put(4, self.a, (0, 3, 1), 1, 0)
        self.got(2, self.b, (3, 0, 0))
        self.put(6, self.b, (3, 0, 1), 0, 1)
        self.got(1, self.a, (0, 1, 0))
        self.put(5, self.a, (0, 1, 2), -1, 0)
        self.got(3, self.b, (1, 0, 0))
        self.put(7, self.b, (1, 0, 2), 0, -1)

    def b0(self):
        self.got(4, self.a, (0, 2, 1))
        self.got(5, self.a, (0, 2, 2))
        self.put(8, self.a, (0, None, 0), 0, 1)
        self.put(9, self.a, (0, None, 0), 0, -1)
        self.got(6, self.b, (2, 0, 1))
        self.got(7, self.b, (2, 0, 2))
        self.put(10, self.b, (None, 0, 0), 1, 0)
        self.put(11, self.b, (None, 0, 0), -1, 0)

    def b1(self):
        self.got(8, self.a, (3, None, 0))
        self.put(12, self.a, (3, None, 1), 0, 1)
        self.got(10, self.b, (None, 3, 0))
        self.put(14, self.b, (None, 3, 1), 1, 0)
        self.got(9, self.a, (1, None, 0))
        self.put(13, self.a, (1, None, 2), 0, -1)
        self.got(11, self.b, (None, 1, 0))
        self.put(15, self.b, (None, 1, 2), -1, 0)

    def end(self):
        self.got(12, self.a, (2, None, 1))
        self.got(13, self.a, (2, None, 2))
        self.got(14, self.b, (None, 2, 1))
        self.got(15, self.b, (None, 2, 2))

    def sent(self):
        for copy in self.sends:
            copy.sent()


class Panel(Plane):
    def cut0(self, d):
        if d == 2:
            self.got(4, self.a, (0, 2, 1))
            self.got(5, self.a, (0, 2, 2))
            self.got(6, self.b, (2, 0, 1))
            self.got(7, self.b, (2, 0, 2))
        n = 8 + 8 * d
        self.put(n, self.a, (0, d, 0), 0, 1)
        self.put(n + 1, self.a, (0, d, 0), 0, -1)
        self.put(n + 2, self.b, (d, 0, 0), 1, 0)
        self.put(n + 3, self.b, (d, 0, 0), -1, 0)

    def cut1(self, d):
        n = 8 + 8 * d
        self.got(n, self.a, (3, d, 0))
        self.put(n + 4, self.a, (3, d, 1), 0, 1)
        self.got(n + 2, self.b, (d, 3, 0))
        self.put(n + 6, self.b, (d, 3, 1), 1, 0)
        self.got(n + 1, self.a, (1, d, 0))
        self.put(n + 5, self.a, (1, d, 2), 0, -1)
        self.got(n + 3, self.b, (d, 1, 0))
        self.put(n + 7, self.b, (d, 1, 2), -1, 0)

    def end(self):
        for d in (0, 1, 3, 2):
            n = 8 + 8 * d
            self.got(n + 4, self.a, (2, d, 1))
            self.got(n + 5, self.a, (2, d, 2))
            self.got(n + 6, self.b, (d, 2, 1))
            self.got(n + 7, self.b, (d, 2, 2))


class Gather:
    def __init__(self, z, q, c, buf, send, recv):
        self.z, self.q, self.c, self.buf, self.send, self.recv = z, q, c, buf, send, recv
        self.sends = []

    def copy(self, n, chunk, dz):
        def make():
            to = lax.rem(self.z + dz + Z, Z)
            view = self.buf.at[lax.rem(self.z + chunk + Z, Z)]
            return view, view, self.send.at[n], self.recv.at[n], (to * 2 + self.q, self.c)
        return Copy(make)

    def put(self, n, chunk, dz):
        copy = self.copy(n, chunk, dz)
        copy.start()
        self.sends.append(copy)

    def got(self, n, chunk):
        self.copy(n, chunk, 0).came()

    def first(self):
        self.put(0, 0, 2)
        self.put(8, 0, -2)
        self.put(4, 0, 1)
        self.put(11, 0, -1)

    def step(self, k):
        self.got(k - 1, -2 * k)
        self.put(k, -2 * k, 2)
        self.put(4 + k, -2 * k, 1)
        self.got(8 + k - 1, 2 * k)
        if k < 3:
            self.put(8 + k, 2 * k, -2)
        self.put(11 + k, 2 * k, -1)

    def end(self):
        self.got(3, -8)
        for k in range(4):
            self.got(4 + k, -2 * k - 1)
            self.got(11 + k, 2 * k + 1)

    def sent(self):
        for copy in self.sends:
            copy.sent()


class Spread:
    def __init__(self, z, q, c, buf, send, recv, k):
        self.z, self.q, self.c, self.buf, self.send, self.recv, self.k = z, q, c, buf, send, recv, k
        self.sends = []

    def copy(self, n, chunk, dz, m):
        def make():
            to = lax.rem(self.z + dz + Z, Z)
            view = self.buf.at[self.k, lax.rem(self.z + chunk + Z, Z)]
            n_, m_ = n + 16 * self.k, m + 16 * self.k
            return view, view, self.send.at[n_], self.recv.at[m_], (to * 2 + self.q, self.c)
        return Copy(make)

    def put(self, n, chunk, dz):
        away = dz - chunk
        copy = self.copy(n, chunk, dz, away - 1 if away > 0 else 7 - away)
        copy.start()
        self.sends.append(copy)

    def got(self, away):
        self.copy(0, -away, 0, away - 1 if away > 0 else 7 - away).came()

    def first(self):
        for n, d in enumerate((4, -4, 3, -3, 2, -2, 1, -1)):
            self.put(n, 0, d)

    def relay(self):
        self.got(4)
        for n, d in enumerate((4, 3, 2, 1)):
            self.put(8 + n, -4, d)
        self.got(-4)
        for n, d in enumerate((3, 2, 1)):
            self.put(12 + n, 4, -d)

    def end(self):
        for d in (1, 2, 3, 5, 6, 7, 8):
            self.got(d)
        for d in (1, 2, 3, 5, 6, 7):
            self.got(-d)

    def sent(self):
        for copy in self.sends:
            copy.sent()


class Reduce:
    def __init__(self, z, q, c, mine, slots, send, recv):
        self.z, self.q, self.c, self.mine, self.slots, self.send, self.recv = z, q, c, mine, slots, send, recv
        self.sends = []

    def put(self, n, d, dz, slot, i):
        def make():
            to = lax.rem(self.z + dz + Z, Z)
            return self.mine.at[d % Z], self.slots[slot].at[i], self.send.at[n], self.recv.at[n], (to * 2 + self.q, self.c)
        copy = Copy(make)
        copy.start()
        self.sends.append(copy)

    def got(self, n, slot, i):
        view = lambda: self.slots[slot].at[i]
        Copy(lambda: (view(), view(), self.send.at[n], self.recv.at[n], (self.z * 2 + self.q, self.c))).came()
        return self.slots[slot][i]

    def first(self):
        self.put(0, 8, 2, 0, 0)
        self.put(4, 7, 1, 1, 0)
        self.put(11, -7, -1, 3, 0)

    def rest(self):
        for i, d in ((1, 5), (2, 3), (3, 1)):
            self.put(4 + i, d, 1, 1, i)
            self.put(11 + i, -d, -1, 3, i)

    def left(self):
        self.mine[10] += self.got(11, 3, 0)
        self.put(8, -6, -2, 2, 0)

    def round(self, k):
        d = 8 - 2 * k
        one = self.got(k - 1, 0, k - 1)
        self.mine[d] += one + self.got(4 + k - 1, 1, k - 1)
        self.put(k, d, 2, 0, k)
        if k < 3:
            d = 2 * k - 8 + 2
            one = self.got(8 + k - 1, 2, k - 1)
            self.mine[d % Z] += one + self.got(11 + k, 3, k)
            self.put(8 + k, d, -2, 2, k)

    def total(self):
        one = self.got(3, 0, 3) + self.got(7, 1, 3)
        two = self.got(10, 2, 2) + self.got(14, 3, 3)
        return self.mine[0] + (one + two)

    def sent(self):
        for copy in self.sends:
            copy.sent()


def kernel(
    slot_ref, flag_ref, rhs_ref, panel_ref, diag_ref, out_ref,
    full, mine0, other0, mine1, other1, minep, otherp, far_r, near_r, far_l, near_l, pfar_r, pnear_r, pfar_l, pnear_l,
    hop_r, hop_l, dz, ee, p10, b0, b1c, b1, chunk1, x0, x1, xh, xl,
    p_send, p_recv, e_send, e_recv, t_send, t_recv, r0_send, r0_recv, g0_send, g0_recv, y_send, y_recv,
    r1_send, r1_recv, rp_send, rp_recv, g1_send, g1_recv, gd_send, gd_recv, m_send, m_recv, f_send, f_recv,
):
    r, c = lax.axis_index("row"), lax.axis_index("col")
    z, q = r // 2, lax.rem(r, 2)
    y, x = c // S, lax.rem(c, S)
    pair = (z * 2 + 1 - q, c)

    def turn(a, n):
        return lax.rem(a + 2 * n, n)

    barrier = pltpu.get_barrier_semaphore()

    def hello(device):
        pl.semaphore_signal(barrier, inc=1, device_id=device, device_id_type=MESH)

    for dy, dx in ((0, 1), (0, -1), (1, 0), (-1, 0)):
        hello((r, turn(y + dy, S) * S + turn(x + dx, S)))
    hello(pair)
    for dist in (1, -1, 2, -2):
        hello((turn(z + dist, Z) * 2 + q, c))

    @pl.when(q == 0)
    def _():
        for dist in (3, -3, 4, -4):
            hello((lax.rem(z + dist + Z, Z) * 2, c))

    held = slot_ref[r]
    is0 = jnp.where(held == 0, 1.0, 0.0).astype(F32)
    is1 = jnp.where(held == 1, 1.0, 0.0).astype(F32)
    f0 = flag_ref[0, 0].astype(F32)
    f1 = flag_ref[0, 1].astype(F32)

    def keep(mark, a, b):
        return jnp.where(jnp.full(a.shape, mark, F32) > 0.5, a, b)

    def mask0(d, _):
        j = lax.rem(z + d, Z)
        rows = rhs_ref[j // 4, lax.rem(j, 4)]
        mine0[d] = keep(is0, rows, jnp.zeros_like(rows))
        return 0

    def mask1(d, _):
        j = lax.rem(z + d, Z)
        t, h = j // 2, lax.rem(j, 2)
        block = panel_ref[0, pl.ds(pl.multiple_of(t * 8, 8), 8), :] * f0
        minep[d] = keep(is1, block, jnp.zeros_like(block))
        for k in range(16):
            rows = rhs_ref[k // 4, k % 4, pl.ds(pl.multiple_of(t * 8, 8), 8), pl.ds(pl.multiple_of(h * 128, 128), 128)]
            mine1[d, 8 * k : 8 * k + 8, :] = keep(is1, rows, jnp.zeros_like(rows))
        return 0

    lax.fori_loop(0, Z, mask0, 0)
    lax.fori_loop(0, Z, mask1, 0)
    for k in range(2):
        full[k, y, x] = panel_ref[k]

    @pl.when(q == 0)
    def _():
        pl.semaphore_wait(barrier, 13)

    @pl.when(q == 1)
    def _():
        pl.semaphore_wait(barrier, 9)

    place = (r, y, x)

    def half(lo, hi, k):
        def piece(yy, xx, part):
            mid = (lo + hi) // 2
            rows = pl.ds(*((lo, hi - lo), (lo, mid - lo), (mid, hi - mid))[part])
            yy = slice(None) if yy is None else yy
            xx = slice(None) if xx is None else xx
            return full.at[k, yy, xx, rows, :]
        return piece

    def columns(buf, lo, hi, k=None):
        def piece(yy, xx, part):
            mid = (lo + hi) // 2
            cols = pl.ds(*((lo, hi - lo), (lo, mid - lo), (mid, hi - mid))[part])
            yy = slice(None) if yy is None else yy
            xx = slice(None) if xx is None else xx
            return buf.at[yy, xx, :, cols] if k is None else buf.at[k, yy, xx, :, cols]
        return piece

    def planes():
        return [Panel(place, half(0, 32, k), half(32, 64, k), p_send, p_recv, 40 * k) for k in range(2)]

    diags = [Plane(place, columns(ee, 0, 2560, k), columns(ee, 2560, 5120, k), e_send, e_recv, 16 * k) for k in range(2)]
    tenth = Plane(place, columns(p10, 0, 512), columns(p10, 512, 1024), t_send, t_recv)
    reduce0 = Reduce(z, q, c, mine0, (far_r, near_r, far_l, near_l), r0_send, r0_recv)
    reducep = Reduce(z, q, c, minep, (pfar_r, pnear_r, pfar_l, pnear_l), rp_send, rp_recv)
    gather0 = Gather(z, q, c, b0, g0_send, g0_recv)
    gather1 = Gather(z, q, c, b1c, g1_send, g1_recv)
    spreads = [Spread(z, q, c, dz, gd_send, gd_recv, k) for k in range(2)]

    def give(n, src, dst, send=f_send, recv=f_recv):
        return Copy(lambda: (src(), dst(), send.at[n], recv.at[n], pair))

    groups = ((6, 5), (11, 5), (0, 6))
    merges = [
        give(i, lambda g=g: mine0.at[pl.ds(*g)], lambda g=g: other0.at[pl.ds(*g)], m_send, m_recv)
        for i, g in enumerate(groups)
    ]
    mergep = give(3, lambda: minep, lambda: otherp, m_send, m_recv)
    merge1 = give(4, lambda: mine1, lambda: other1, m_send, m_recv)
    owner = c // 8

    def diag_piece():
        first_row = pl.multiple_of(lax.rem(c // 2, 4) * 8, 8)
        first_col = pl.multiple_of(lax.rem(c, 2) * (z // 4 + 1) * 128, 128)
        return slice(None), pl.ds(first_row, 8), pl.ds(first_col, 512)

    give_dz = give(1, lambda: diag_ref.at[diag_piece()], lambda: dz.at[:, z])
    give_p10 = give(2, lambda: p10, lambda: p10)
    give_chunk = give(3, lambda: mine1.at[0], lambda: chunk1)

    def give_rows(k, d):
        a = lambda: ee.at[k, lax.rem(y + d, S), :, :, 0:2560]
        b = lambda: ee.at[k, :, lax.rem(x + d, S), :, 2560:5120]
        return [give(8 * k + 2 * d, a, a, y_send, y_recv), give(8 * k + 2 * d + 1, b, b, y_send, y_recv)]

    give_ee = [sum((give_rows(k, d) for d in range(S)), []) for k in range(2)]
    give_x0 = give(5, lambda: x0, lambda: x0)
    give_x1 = [give(6 + i, lambda i=i: x1.at[i], lambda i=i: x1.at[i]) for i in range(4)]

    sums1 = []

    def hop(t):
        def put(n, d, dz_, buf, i):
            copy = Copy(lambda: (mine1.at[d % Z], buf.at[i], r1_send.at[n], r1_recv.at[n], (turn(z + dz_, Z) * 2 + q, c)))
            copy.start()
            sums1.append(copy)

        def got(n, buf, i):
            Copy(lambda: (buf.at[i], buf.at[i], r1_send.at[n], r1_recv.at[n], (r, c))).came()
            return buf[i]

        if t:
            mine1[8 - t] += got(t - 1, hop_r, t - 1)
        if t < 8:
            put(t, 8 - t, 1, hop_r, t)
        if 0 < t < 8:
            mine1[(t - 7) % Z] += got(8 + t - 1, hop_l, t - 1)
        if t < 7:
            put(8 + t, t - 7, -1, hop_l, t)

    def take(load, n):
        for i in range(1024 // n):
            high, low_part = split(load(i))
            xh[n * i : n * i + n, :] = high
            xl[n * i : n * i + n, :] = low_part

    def unit(d, load):
        top_rows = load(lax.rem(y + d, S), slice(None), slice(0, 32))
        bottom_rows = load(slice(None), lax.rem(x + d, S), slice(32, 64))
        return jnp.concatenate([v.reshape(128, v.shape[-1]) for v in (top_rows, bottom_rows)], axis=0)

    def store(d, value):
        out_ref[lax.rem(y + d, S), :, 0:32, :] = value[:128].reshape(4, 32, 256)
        out_ref[:, lax.rem(x + d, S), 32:64, :] = value[128:].reshape(4, 32, 256)

    def product(k, d):
        return dot3(unit(d, lambda *at: full[(k, *at, slice(None))]), xh[...], xl[...])

    def step0(d):
        store(d, unit(d, lambda *at: rhs_ref[(*at, slice(None))]) - f0 * product(0, d))

    def step1(d):
        value = unit(d, lambda *at: out_ref[(*at, slice(None))]) - f1 * product(1, d)
        solved0 = unit(d, lambda *at: x0[(*at, slice(None))])
        solved1 = unit(d, lambda *at: x1[(*at, slice(None))])
        store(d, keep(is0, solved0, keep(is1, solved1, value)))

    def solve(k, done):
        off = 0
        for g in range(4):
            width = 128 * (g + 1)
            value = None
            for side in range(2):
                rows_ = []
                for i in range(4):
                    parts = [ee[k, :, 2 * o + side, :, off + width * i : off + width * i + width] for o in range(2)]
                    rows_.append(jnp.stack(parts, axis=1).reshape(64, width))
                lo = width * side
                term = dot3(jnp.concatenate(rows_, axis=0), xh[lo : lo + width, :], xl[lo : lo + width, :])
                value = term if value is None else value + term
            off += 4 * width
            done(g, value.reshape(4, 64, 256))

    @pl.when(q == 1)
    def _():
        panels = planes()
        panels[0].a0()
        mergep.start()

        @pl.when(owner == 1)
        def _():
            give_dz.start()

        merge1.start()
        panels[1].a0()

        def merge(i):
            merges[i].came()
            lo, n = groups[i]
            for d in range(lo, lo + n):
                mine0[d] += other0[d]

        merge(0)
        reduce0.first()
        merge(1)
        merge(2)
        reduce0.rest()
        reduce0.left()
        reduce0.round(1)
        panels[0].a1()
        panels[1].a1()
        reduce0.round(2)
        panels[0].cut0(0)
        reduce0.round(3)
        panels[0].cut0(1)
        b0[z] = reduce0.total()
        gather0.first()
        panels[0].cut0(3)
        gather0.step(1)
        panels[0].cut0(2)
        gather0.step(2)
        panels[0].cut1(0)
        panels[1].cut0(0)
        gather0.step(3)
        panels[0].cut1(1)
        panels[1].cut0(1)
        gather0.end()
        take(lambda i: b0[i], 64)
        for copy in give_ee[0]:
            copy.came()

        def done0(g, value):
            x0[g] = value

        solve(0, done0)
        give_x0.start()
        take(lambda i: x0[i].reshape(256, 256), 256)
        panels[0].cut1(3)
        panels[1].cut0(3)
        give_p10.came()
        give_chunk.came()
        h = pl.multiple_of(lax.rem(z, 2) * 128, 128)
        b1c[z] = chunk1[...] - dot3(p10[...].reshape(128, 1024), xh[:, pl.ds(h, 128)], xl[:, pl.ds(h, 128)])
        gather1.first()
        panels[0].cut1(2)
        panels[1].cut0(2)
        step0(0)
        gather1.step(1)
        panels[1].cut1(0)
        step0(1)
        gather1.step(2)
        panels[1].cut1(1)
        step0(3)
        gather1.step(3)
        panels[1].cut1(3)
        panels[0].end()
        step0(2)
        gather1.end()
        for t in range(8):
            for h in range(2):
                for k in range(16):
                    b1[64 * k + 8 * t : 64 * k + 8 * t + 8, 128 * h : 128 * h + 128] = b1c[2 * t + h, 8 * k : 8 * k + 8, :]
        take(lambda i: b1[256 * i : 256 * i + 256, :], 256)
        panels[1].cut1(2)
        for copy in give_ee[1]:
            copy.came()

        def done1(g, value):
            x1[g] = value
            give_x1[g].start()

        solve(1, done1)
        take(lambda i: x1[i].reshape(256, 256), 256)
        for d in (0, 1, 3):
            step1(d)
        panels[1].end()
        step1(2)
        for part in panels + [reduce0, gather0, gather1]:
            part.sent()
        for copy in [mergep, merge1, give_x0] + give_x1:
            copy.sent()

        @pl.when(owner == 1)
        def _():
            give_dz.sent()

    @pl.when(q == 0)
    def _():
        panels = planes()

        def pack(k):
            off = 0
            for i in range(16):
                width = 128 * (i // 4 + 1)
                ee[k, y, x, :, off : off + width] = dz[k, i, :, 0:width]
                off += width

        def hand(k, *distances):
            for d in distances:
                for copy in give_ee[k][2 * d : 2 * d + 2]:
                    copy.start()

        for copy in merges:
            copy.start()

        @pl.when(owner == 0)
        def _():
            dz[:, z] = diag_ref[diag_piece()]

        @pl.when(owner == 1)
        def _():
            give_dz.came()

        spreads[0].first()
        panels[0].a0()
        mergep.came()
        minep[...] += otherp[...]
        reducep.first()
        reducep.rest()
        panels[1].a0()
        merge1.came()
        mine1[...] += other1[...]
        hop(0)
        reducep.left()
        spreads[0].relay()
        reducep.round(1)
        panels[0].a1()
        hop(1)
        panels[1].a1()
        spreads[0].end()
        pack(0)
        diags[0].a0()
        reducep.round(2)
        hop(2)
        panels[0].cut0(0)
        diags[0].a1()
        reducep.round(3)
        hop(3)
        spreads[1].first()
        panels[0].cut0(1)
        diags[0].b0()
        p10[y, x] = reducep.total()
        tenth.a0()
        hop(4)
        panels[0].cut0(3)
        spreads[1].relay()
        tenth.a1()
        diags[0].b1()
        hand(0, 0, 1, 3)
        hop(5)
        panels[0].cut0(2)
        tenth.b0()
        diags[0].end()
        hand(0, 2)
        hop(6)
        spreads[1].end()
        pack(1)
        diags[1].a0()
        panels[0].cut1(0)
        panels[1].cut0(0)
        tenth.b1()
        hop(7)
        diags[1].a1()
        panels[0].cut1(1)
        panels[1].cut0(1)
        tenth.end()
        give_p10.start()
        hop(8)
        give_chunk.start()
        diags[1].b0()
        panels[0].cut1(3)
        panels[1].cut0(3)
        diags[1].b1()
        hand(1, 0, 1, 3)
        panels[0].cut1(2)
        panels[1].cut0(2)
        panels[1].cut1(0)
        diags[1].end()
        hand(1, 2)
        give_x0.came()
        take(lambda i: x0[i].reshape(256, 256), 256)
        step0(0)
        panels[1].cut1(1)
        step0(1)
        panels[1].cut1(3)
        step0(3)
        panels[1].cut1(2)
        panels[0].end()
        step0(2)
        for copy in give_x1:
            copy.came()
        take(lambda i: x1[i].reshape(256, 256), 256)
        for d in (0, 1, 3):
            step1(d)
        panels[1].end()
        step1(2)
        for part in panels + diags + spreads + [reducep, tenth]:
            part.sent()
        for copy in merges + sums1 + give_ee[0] + give_ee[1] + [give_p10, give_chunk]:
            copy.sent()


def shards(rhs, panel, diag_inverse, flags, slot_block):
    vmem = lambda *shape, dtype=F32: pltpu.VMEM(shape, dtype)
    dma = lambda *shape: pltpu.SemaphoreType.DMA(shape)
    scratch = [
        vmem(2, 4, 4, 64, 1024),
        vmem(16, 64, 256), vmem(16, 64, 256),
        vmem(16, 128, 128), vmem(16, 128, 128),
        vmem(16, 8, 1024), vmem(16, 8, 1024),
        vmem(4, 64, 256), vmem(4, 64, 256), vmem(3, 64, 256), vmem(4, 64, 256),
        vmem(4, 8, 1024), vmem(4, 8, 1024), vmem(3, 8, 1024), vmem(4, 8, 1024),
        vmem(8, 128, 128), vmem(7, 128, 128),
        vmem(2, 16, 8, 512),
        vmem(2, 4, 4, 8, 5120),
        vmem(4, 4, 8, 1024),
        vmem(16, 64, 256),
        vmem(16, 128, 128),
        vmem(1024, 256),
        vmem(128, 128),
        vmem(4, 4, 64, 256),
        vmem(4, 4, 64, 256),
        vmem(1024, 256, dtype=BF16), vmem(1024, 256, dtype=BF16),
        dma(80), dma(80), dma(32), dma(32),
    ]
    scratch += [dma(16) for _ in range(14)]
    scratch += [dma(32), dma(32)]
    scratch += [dma(5), dma(5), dma(10), dma(10)]
    whole = pl.BlockSpec(memory_space=pltpu.VMEM)
    scalar = pl.BlockSpec(memory_space=pltpu.SMEM)
    result = pl.pallas_call(
        kernel,
        out_shape=jax.ShapeDtypeStruct((4, 4, 64, 256), F32),
        in_specs=[scalar, scalar, whole, whole, whole],
        out_specs=whole,
        scratch_shapes=scratch,
        name="substitution",
        compiler_params=pltpu.CompilerParams(collective_id=0, has_side_effects=True, vmem_limit_bytes=56 << 20),
    )(slot_block, flags, rhs.reshape(4, 4, 64, 256), panel[0], diag_inverse)
    return result.reshape(1, 1024, 256)


def solution(mesh):
    in_specs = (
        P("row", None, "col"),
        P("row", None, "col", None),
        P(None, "row", None),
        P("row", None),
        P(),
    )
    out_specs = P("row", None, "col")
    return jax.shard_map(shards, mesh=mesh, in_specs=in_specs, out_specs=out_specs, check_vma=False)
```

time: 743 us -> 96.4 us (0.13)
  waiting for transfers between devices: 699 us -> 0 us
  Pallas kernels: 0 us -> 93.9 us
  matrix products: 20.5 us -> 0 us
  between operations: 16.1 us -> 0.01 us
    psum x2 -> x0, waiting for transfers between devices: 426 us -> none  [broadcast(): return lax.psum(jnp.where(mine, shard, jnp.zeros_like(shard)), axis)]
    all_gather x4 -> x0, waiting for transfers between devices: 273 us -> none  [the longest x2 141 us: shards(): block_x = lax.all_gather(share, 'row', axis=0, tiled=True)]
    pallas_call x0 -> x1, Pallas kernels: none -> 93.9 us  [shards(): pl.pallas_call(kernel, out_shape=jax.ShapeDtypeStruct((4, 4, 64, 256), F3...]
    dot_general x4 -> x0, matrix products: 20.5 us -> none  [the longest x2 15.6 us: shards(): jnp.dot(lax.all_gather(panel[0, step], 'col', axis=0, tiled=True), block_...]
  transfers between devices with their start and end apart: 6 -> 0, of which waited for: 6 -> 0; matrix products, arithmetic and copies ran while one was open for 1% -> 0% of each run, Pallas kernels for 0% -> 0%
where the time goes in v2:
time: 96.4 us; the launch traced here: 96.2 us
  Pallas kernels  93.9 us (97%)
  local copies, waits for them, and re-layouts  2.26 us (2%)
    pallas_call x1, Pallas kernels, shards(): pl.pallas_call(kernel, out_shape=jax.ShapeDtypeStruct((4, 4, 64, 256), F3...  93.9 us
    unnamed x1, local copies, waits for them, and re-layouts  2.26 us

profile of v2, /device:TPU:1, one launch (start us, length us, event | category | flops | bytes accessed | tf_op | source)
XLA Modules:
  0.0 96.2 jit_solution(16774714234593266047)
XLA Ops:
  0.0 93.9 %substitution.1 = f32[4,4,64,256]{3,2,1,0:T(8,128)} custom-call(s32[32]{0:T(128)} %slot_ref.1, s32[1,2]{1,0:T(1,128)} %flag_ref.1, f32[4,4,64,256]{3,2,1,0:T(8,128)} %bitcast.4, f32[2,64,1024]{2,1,0:T(8,128)} %bitcast.5, f32[2,32,1024]{2,1,0:T(8,128)} %diag_ref.1), custom_call_target="tpu_custom_call" | custom-call | tf_op jit(solution)/shard_map/substitution/pallas_call | solution.py:740
  93.9 2.3 %copy.7 = f32[1,1024,256]{2,1,0:T(8,128)} copy(f32[1,1024,256]{2,1,0:T(8,128)} %bitcast.3) | data formatting | bytes 2097152

commit v3 on v2

--- a/solution.py
+++ b/solution.py
@@ -709,6 +709,10 @@
             copy.sent()
 
 
+def hand_out(value_ref, result_ref):
+    result_ref[...] = value_ref[...]
+
+
 def shards(rhs, panel, diag_inverse, flags, slot_block):
     vmem = lambda *shape, dtype=F32: pltpu.VMEM(shape, dtype)
     dma = lambda *shape: pltpu.SemaphoreType.DMA(shape)
@@ -746,7 +750,15 @@
         name="substitution",
         compiler_params=pltpu.CompilerParams(collective_id=0, has_side_effects=True, vmem_limit_bytes=56 << 20),
     )(slot_block, flags, rhs.reshape(4, 4, 64, 256), panel[0], diag_inverse)
-    return result.reshape(1, 1024, 256)
+    block = pl.BlockSpec((256, 256), lambda i: (i, 0))
+    return pl.pallas_call(
+        hand_out,
+        grid=(4,),
+        out_shape=jax.ShapeDtypeStruct((1024, 256), F32),
+        in_specs=[block],
+        out_specs=block,
+        name="hand_out",
+    )(result.reshape(1024, 256)).reshape(1, 1024, 256)
 
 
 def solution(mesh):

time: 96.4 us -> 97.5 us (1.011)
  Pallas kernels: 93.9 us -> 97.3 us
  local copies, waits for them, and re-layouts: 2.26 us -> 0 us
    pallas_call x0 -> x1, Pallas kernels: none -> 3.37 us  [shards(): pl.pallas_call(hand_out, grid=(4,), out_shape=jax.ShapeDtypeStruct((1024,...]
    unnamed x1 -> x0, local copies, waits for them, and re-layouts: 2.26 us -> none
where the time goes in v3:
time: 97.5 us; the launch traced here: 97.3 us
  Pallas kernels  97.3 us (100%)
    pallas_call x1, Pallas kernels, shards(): pl.pallas_call(kernel, out_shape=jax.ShapeDtypeStruct((4, 4, 64, 256), F3...  93.9 us
    pallas_call x1, Pallas kernels, shards(): pl.pallas_call(hand_out, grid=(4,), out_shape=jax.ShapeDtypeStruct((1024,...  3.37 us

profile of v3, /device:TPU:1, one launch (start us, length us, event | category | flops | bytes accessed | tf_op | source)
XLA Modules:
  0.0 97.3 jit_solution(17160971202261688334)
XLA Ops:
  0.0 93.9 %substitution.1 = f32[4,4,64,256]{3,2,1,0:T(8,128)} custom-call(s32[32]{0:T(128)} %slot_ref.1, s32[1,2]{1,0:T(1,128)} %flag_ref.1, f32[4,4,64,256]{3,2,1,0:T(8,128)} %bitcast.5, f32[2,64,1024]{2,1,0:T(8,128)} %bitcast.6, f32[2,32,1024]{2,1,0:T(8,128)} %diag_ref.1), custom_call_target="tpu_custom_call" | custom-call | tf_op jit(solution)/shard_map/substitution/pallas_call | solution.py:744
  93.9 3.4 %hand_out.1 = f32[1024,256]{1,0:T(8,128)} custom-call(f32[1024,256]{1,0:T(8,128)} %bitcast.4), custom_call_target="tpu_custom_call" | custom-call | tf_op jit(solution)/shard_map/hand_out/pallas_call | solution.py:754
